TPU v7x, 32 devices: a whole 2x2x4 slice. The times are simulated.
32 devices in a mesh: mode: 4 (over x, core), batch: 4 (over z), cores: 2 (over y).
Axes of the slice: x: 2, y: 2, z: 4, core: 2. Of those that a mesh axis runs over, the one named last changes fastest.
Arguments:
- fields: bfloat16 [4, 20, 1024, 1024], P('batch', None, ('mode', 'cores')), may hold values from -6 to 6
- lift_weight: bfloat16 [20, 128], replicated, may hold values from -1.25 to 1.25
- lift_bias: float32 [128], replicated, may hold values from -3 to 3
- first_core: bfloat16 [128, 32, 32], P('batch'), may hold values from -1 to 1
- second_core: bfloat16 [128, 32, 32], P(('mode', 'cores')), may hold values from -1 to 1
- input_core: bfloat16 [128, 32, 32], P('batch'), may hold values from -0.09375 to 0.09375
- output_core: bfloat16 [128, 2, 32, 32], P('batch'), may hold values from -3 to 3
- skip_weight: bfloat16 [128, 128], replicated, may hold values from -0.5 to 0.5
- skip_bias: float32 [128], replicated, may hold values from -3 to 3
- out_weight: bfloat16 [128, 20], replicated, may hold values from -0.5 to 0.5
- out_bias: float32 [20], replicated, may hold values from -3 to 3
Outputs:
- updated: bfloat16 [4, 20, 1024, 1024], P('batch', None, ('mode', 'cores'))
All inputs are finite; a program needn't handle non-finite values.
Results may differ from a plain program's by a relative error of at most 0.012.
Values may be sent and summed in bfloat16 or wider, within the bound.
A program may use at most 256 MiB of HBM per device.

v0:
```python
import math

import jax
import jax.numpy as jnp
from jax import lax
from jax.sharding import PartitionSpec as P

NX = 1024
NY = 1024
MX = 128
MY = 128


TWO_PI = 2.0 * math.pi


def wave_pair(waves, points, length):
    phase_step = waves[:, None] * points[None, :] % length
    angles = phase_step.astype(jnp.float32) * (TWO_PI / length)
    return (jnp.cos(angles), jnp.sin(angles))


def width_forward(length, wave_count):
    points = jnp.arange(length, dtype=jnp.int32)
    waves = jnp.arange(wave_count, dtype=jnp.int32)
    cosines, sine_part = wave_pair(points, waves, length)
    stacked = jnp.stack([cosines, -sine_part], axis=1) / math.sqrt(length)
    return stacked.astype(jnp.bfloat16)


def height_forward(row_index, wave_count, length):
    waves = jnp.arange(wave_count, dtype=jnp.int32) - wave_count // 2
    cosines, sine_part = wave_pair(waves, row_index, length)
    upper = jnp.stack([cosines, sine_part], axis=1)
    lower = jnp.stack([-sine_part, cosines], axis=1)
    return (jnp.stack([upper, lower], axis=0) / math.sqrt(length)).astype(jnp.bfloat16)


def height_inverse(row_index, wave_count, length):
    waves = jnp.arange(wave_count, dtype=jnp.int32) - wave_count // 2
    cosines, sine_part = wave_pair(row_index, waves, length)
    upper = jnp.stack([cosines, -sine_part], axis=1)
    lower = jnp.stack([sine_part, cosines], axis=1)
    return (jnp.stack([upper, lower], axis=0) / math.sqrt(length)).astype(jnp.bfloat16)


def width_inverse(waves, length):
    points = jnp.arange(length, dtype=jnp.int32)
    cosines, sine_part = wave_pair(waves, points, length)
    weight = jnp.where(waves == 0, 1.0, 2.0).astype(jnp.float32)[:, None]
    stacked = jnp.stack([cosines * weight, -sine_part * weight], axis=0) / math.sqrt(length)
    return stacked.astype(jnp.bfloat16)


def bias_modes(lift_bias, wave_index, length):
    real_row = (
        jnp.where(wave_index == 0, 1.0, 0.0).astype(jnp.float32)[:, None]
        * (math.sqrt(length) * lift_bias)[None, :]
    )
    return jnp.stack([real_row, jnp.zeros_like(real_row)], axis=0)


def lift_modes(modes, lift_weight, lift_bias, wave_index):
    lifted_modes = jnp.einsum(
        "fabpmv,vc->fabpmc", modes, lift_weight, preferred_element_type=jnp.float32
    )
    return (lifted_modes + bias_modes(lift_bias, wave_index, NY)).astype(jnp.bfloat16)


def grid_rows(stored, row_count, holder_count):
    return stored % row_count * holder_count + stored // row_count


def shards(
    fields,
    lift_weight,
    lift_bias,
    first_core,
    second_core,
    input_core,
    output_core,
    skip_weight,
    skip_bias,
    out_weight,
    out_bias,
):
    mode_count = lax.axis_size("mode")
    core_count = lax.axis_size("cores")
    row_count = fields.shape[2]
    block_size = second_core.shape[0]
    block_start = (lax.axis_index("mode") * core_count + lax.axis_index("cores")) * block_size
    local_waves = block_start + jnp.arange(block_size, dtype=jnp.int32)
    lifted = (
        jnp.einsum("fvxy,vc->fxyc", fields, lift_weight, preferred_element_type=jnp.float32)
        + lift_bias
    ).astype(jnp.bfloat16)
    field_modes = jnp.einsum(
        "fvxy,ypk->fxpkv", fields, width_forward(NY, MY), preferred_element_type=jnp.float32
    ).astype(jnp.bfloat16)
    field_modes = field_modes[:, None]
    gathered = (
        lax.all_gather(first_core, "batch", axis=0, tiled=True),
        lax.all_gather(input_core, "batch", axis=0, tiled=True),
        lax.all_gather(output_core, "batch", axis=0, tiled=True),
    )
    first_whole, input_whole, output_whole = gathered
    mode_factor = jnp.einsum(
        "kab,mbd->kmad", first_whole, second_core, preferred_element_type=jnp.float32
    ).astype(jnp.bfloat16)
    arrived = lax.all_to_all(
        field_modes, ("mode", "cores"), split_axis=4, concat_axis=2, tiled=True
    )
    rows_held = jnp.arange(NX, dtype=jnp.int32)[None, :]
    by_mode = lift_modes(arrived, lift_weight, lift_bias, local_waves)
    lead_rows = rows_held.shape[0]
    side_rows = rows_held.shape[1]
    flat_rows = grid_rows(rows_held.reshape(-1), row_count, mode_count * core_count)
    height_table = height_forward(flat_rows, MX, NX).reshape(2, MX, 2, lead_rows, side_rows)
    spectrum = jnp.einsum(
        "qkpab,fabpmc->fqkmc", height_table, by_mode, preferred_element_type=jnp.float32
    ).astype(jnp.bfloat16)
    projected = jnp.einsum(
        "fqkmc,cbe->fqkmbe", spectrum, input_whole, preferred_element_type=jnp.float32
    ).astype(jnp.bfloat16)
    carried = jnp.einsum(
        "kmab,fqkmbe->fqkmae", mode_factor, projected, preferred_element_type=jnp.float32
    ).astype(jnp.bfloat16)
    traced = jnp.einsum(
        "fqkmae,osea->fqkmso", carried, output_whole, preferred_element_type=jnp.float32
    )
    real_part = traced[:, 0, :, :, 0, :] - traced[:, 1, :, :, 1, :]
    imaginary = traced[:, 0, :, :, 1, :] + traced[:, 1, :, :, 0, :]
    mixed_modes = jnp.stack([real_part, imaginary], axis=1).astype(jnp.bfloat16)
    height_back = height_inverse(flat_rows, MX, NX).reshape(2, lead_rows, side_rows, 2, MX)
    col_modes = jnp.einsum(
        "pabqk,fqkmc->fabpmc", height_back, mixed_modes, preferred_element_type=jnp.float32
    ).astype(jnp.bfloat16)
    returned = lax.all_to_all(col_modes, ("mode", "cores"), split_axis=2, concat_axis=4, tiled=True)
    waves_held = jnp.arange(MY, dtype=jnp.int32)
    width_back = width_inverse(waves_held, NY)
    spatial = jnp.einsum(
        "fxpmc,pmy->fxyc", returned[:, 0], width_back, preferred_element_type=jnp.float32
    )
    skip_term = jnp.einsum("fxyc,cd->fxyd", lifted, skip_weight, preferred_element_type=jnp.float32)
    active = jax.nn.gelu(spatial + skip_term + skip_bias, approximate=False).astype(jnp.bfloat16)
    result = (
        jnp.einsum("fxyc,cv->fvxy", active, out_weight, preferred_element_type=jnp.float32)
        + out_bias[:, None, None]
    )
    return result.astype(jnp.bfloat16)


def solution(mesh):
    placed = (
        P("batch", None, ("mode", "cores"), None),
        P(),
        P(),
        P("batch", None, None),
        P(("mode", "cores"), None, None),
        P("batch", None, None),
        P("batch", None, None, None),
        P(),
        P(),
        P(),
        P(),
    )
    return jax.shard_map(
        shards,
        mesh=mesh,
        in_specs=placed,
        out_specs=P("batch", None, ("mode", "cores"), None),
        check_vma=False,
    )
```

profile of v0, /device:TPU:0, one launch (start us, length us, event | category | flops | bytes accessed | tf_op | source)
XLA Modules:
  0.0 632.1 jit_solution(4444873286141601486)
XLA Ops:
  0.0 2.1 sine_negate_fusion
  2.1 4.1 fusion.36
  6.1 2.4 copy.49
  8.6 5.2 all-to-all-start
  14.4 1.8 copy.59
  16.3 22.9 %all_gather.10 = bf16[128,32,32]{2,1,0:T(8,128)(2,1)S(1)} all-gather(bf16[32,32,32]{2,1,0:T(8,128)(2,1)} %param.14), channel_id=1, replica_groups=mesh['mode'=4,'batch'=4,'cores'=2] {'batch'}, dimensions={0}, use_global_device_ids=true | all-gather | bytes 327680 | tf_op jit(solution)/shard_map/all_gather | solution.py:102
  39.2 3.3 convert_bitcast_fusion.1
  42.5 23.0 %copy.75 = bf16[128,16,32,32,1]{3,2,4,1,0:T(8,128)(2,1)} copy(bf16[128,16,32,32,1]{0,3,2,1,4:T(8,128)(2,1)} %convert_bitcast_fusion.1) | data formatting | bytes 8388608 | tf_op jit(solution)/shard_map/convert_element_type | solution.py:109
  65.6 24.2 %all_gather.9 = bf16[128,32,32]{2,1,0:T(8,128)(2,1)} all-gather(bf16[32,32,32]{2,1,0:T(8,128)(2,1)} %param.16), channel_id=1, replica_groups=mesh['mode'=4,'batch'=4,'cores'=2] {'batch'}, dimensions={0}, use_global_device_ids=true | all-gather | bytes 327680 | tf_op jit(solution)/shard_map/all_gather | solution.py:103
  89.8 2.1 fusion.87
  92.0 1.6 maximum_bitcast_fusion
  93.5 2.1 fusion.92
  95.6 1.6 maximum_bitcast_fusion.3
  97.2 36.8 %all_gather.11 = bf16[128,2,32,32]{2,0,3,1:T(8,128)(2,1)} all-gather(bf16[32,2,32,32]{2,0,3,1:T(8,128)(2,1)S(1)} %copy.59), channel_id=1, replica_groups=mesh['mode'=4,'batch'=4,'cores'=2] {'batch'}, dimensions={0}, use_global_device_ids=true | all-gather | bytes 655360 | tf_op jit(solution)/shard_map/all_gather | solution.py:104
  134.1 0.8 copy.118
  134.9 0.9 reshape.755
  135.8 8.7 %fusion.39 = bf16[2,128,16,128,1]{1,3,0,2,4:T(8,128)(2,1)S(1)} fusion(f32[2,16,128]{2,0,1:T(2,128)S(1)} %stack.59, bf16[1024,2,16,20]{0,2,3,1:T(8,128)(2,1)S(1)} %reshape.755, f32[1,128,2,1024]{3,1,2,0:T(8,128)} %get-tuple-element.6, f32[1,128,2,1024]{3,1,2,0:T(8,128)} %get-tuple-element.5, bf16[20,128]{1,0:T(8,128)(2,1)} %param.12), kind=kOutput, calls=%fused_computation.50 | convolution fusion | flops 2325741568 | bytes 4477952 | tf_op jit(solution)/shard_map/qkpab,fabpmc->fqkmc/dot_general | solution.py:119
  144.5 6.9 %convolution_convert_fusion = bf16[2,128,16,32,32]{1,4,3,2,0:T(8,128)(2,1)} fusion(bf16[128,32,32,1,1]{2,1,0,4,3:T(8,128)(2,1)} %bitcast.201, bf16[2,128,16,128,1]{1,3,0,2,4:T(8,128)(2,1)S(1)} %fusion.39), kind=kOutput, calls=%fused_computation.36 | convolution fusion | flops 1077936128 | bytes 9699328 | tf_op jit(solution)/shard_map/fqkmc,cbe->fqkmbe/dot_general | solution.py:122
  151.4 54.9 %copy.57 = bf16[2,128,16,32,32]{3,4,0,2,1:T(8,128)(2,1)} copy(bf16[2,128,16,32,32]{1,4,3,2,0:T(8,128)(2,1)} %convolution_convert_fusion) | data formatting | bytes 16777216 | tf_op jit(solution)/shard_map/convert_element_type | solution.py:124
  206.3 28.3 %convert_bitcast_fusion = bf16[2,128,16,32,32,1]{3,4,0,2,1,5:T(8,128)(2,1)} fusion(bf16[2,128,16,32,32]{3,4,0,2,1:T(8,128)(2,1)} %copy.57, bf16[128,16,32,32,1]{3,2,4,1,0:T(8,128)(2,1)} %copy.75), kind=kOutput, calls=%fused_computation.26 | convolution fusion | flops 272629760 | bytes 20971520 | tf_op jit(solution)/shard_map/kmab,fqkmbe->fqkmae/dot_general | solution.py:125
  234.6 47.5 %copy.76 = bf16[2,128,16,32,32,1]{1,4,3,5,2,0:T(8,128)(2,1)} copy(bf16[2,128,16,32,32,1]{3,4,0,2,1,5:T(8,128)(2,1)} %convert_bitcast_fusion) | data formatting | bytes 16777216 | tf_op jit(solution)/shard_map/reshape.14
  282.1 12.4 %convolution_bitcast_fusion = f32[1,2,128,16,2,128]{5,2,4,3,1,0:T(8,128)S(1)} fusion(bf16[2,128,16,32,32,1]{1,4,3,5,2,0:T(8,128)(2,1)} %copy.76, bf16[128,2,32,32]{2,0,3,1:T(8,128)(2,1)} %all_gather.11), kind=kOutput, calls=%fused_computation.40 | convolution fusion | flops 2147483648 | bytes 13107200 | tf_op jit(solution)/shard_map/fqkmae,osea->fqkmso/dot_general | solution.py:128
  294.8 5.6 fusion.21
  300.4 21.3 %copy.65 = bf16[1,1,1024,2,16,128]{5,3,4,1,0,2:T(2,128)(2,1)} copy(bf16[1,1,1024,2,16,128]{2,5,3,4,1,0:T(8,128)(2,1)} %fusion.21) | data formatting | bytes 16777216 | tf_op jit(solution)/shard_map/convert_element_type | solution.py:137
  321.7 5.1 all-to-all-start.1
  326.8 2.1 cosine_multiply_fusion
  328.9 27.3 %fusion.19 = f32[128,1024,128]{2,1,0:T(8,128)} fusion(bf16[20,128,1024]{2,1,0:T(8,128)(2,1)} %bitcast.198, bf16[20,128]{1,0:T(8,128)(2,1)S(1)} %copy-done.4), kind=kOutput, calls=%fused_computation.33 | convolution fusion | flops 671088640 | bytes 72356864 | tf_op jit(solution)/shard_map/fvxy,vc->fxyc/dot_general | solution.py:94
  356.2 63.7 %all-to-all-done.1 = bf16[1,1,1024,2,16,128]{5,3,4,1,0,2:T(2,128)(2,1)} async-done(((bf16[1,1,1024,2,16,128]{5,3,4,1,0,2:T(2,128)(2,1)}), bf16[1,1,1024,2,16,128]{5,3,4,1,0,2:T(2,128)(2,1)}, u32[]{:S(2)}, u32[]{:S(2)}) %all-to-all-start.1) | async-done | bytes 8388640 | tf_op jit(solution)/shard_map/all_to_all | solution.py:138
  420.0 9.1 %copy.66 = bf16[1,1,8,128,2,16,128]{6,5,2,4,3,1,0:T(8,128)(2,1)} copy(bf16[1,1,8,128,2,16,128]{6,4,5,3,2,1,0:T(2,128)(2,1)} %bitcast.50) | data formatting | bytes 16777216 | tf_op jit(solution)/shard_map/all_to_all | solution.py:138
  429.1 26.7 %fusion.75 = f32[1024,128,128,1]{2,0,3,1:T(8,128)} fusion(bf16[128,2,128,128]{3,2,1,0:T(8,128)(2,1)} %bitcast.197, f32[1,128,1024]{1,2,0:T(8,128)S(1)} %get-tuple-element.16, f32[1,128,1024]{1,2,0:T(8,128)S(1)} %get-tuple-element.15), kind=kOutput, calls=%fused_computation.106 | convolution fusion | flops 8590721024 | bytes 76546048 | tf_op jit(solution)/shard_map/fxpmc,pmy->fxyc/dot_general | solution.py:141
  455.8 167.8 %fusion.18 = bf16[1,20,128,1024]{3,1,2,0:T(8,128)(2,1)} fusion(f32[20]{0:T(128)S(1)} %copy-done.7, f32[128]{0:T(128)S(1)} %copy-done.8, f32[1024,128,128,1]{2,0,3,1:T(8,128)} %fusion.75, f32[128,1024,128]{2,1,0:T(8,128)} %fusion.19, f32[128]{0:T(128)S(1)} %copy-done.9, bf16[128,128]{1,0:T(8,128)(2,1)S(1)} %copy-done.5, bf16[128,20]{0,1:T(8,128)(2,1)S(1)} %copy-done.6), kind=kOutput, calls=%fused_computation.32 | convolution fusion | flops 6128926720 | bytes 139499600 | tf_op jit(solution)/shard_map/fxyc,cv->fvxy/dot_general | solution.py:147
  623.6 8.1 %copy.68 = bf16[1,20,128,1024]{3,2,1,0:T(8,128)(2,1)} copy(bf16[1,20,128,1024]{3,1,2,0:T(8,128)(2,1)} %fusion.18) | data formatting | bytes 10485760 | tf_op jit(solution)/shard_map/convert_element_type | solution.py:150
  (30 shorter events, 1.0 us)
Async XLA Ops:
  0.0 39.2 %copy-start = (bf16[16,32,32]{2,1,0:T(8,128)(2,1)S(1)}, bf16[16,32,32]{2,1,0:T(8,128)(2,1)}, u32[]{:S(2)}) copy-start(bf16[16,32,32]{2,1,0:T(8,128)(2,1)} %param.15) | copy-start | bytes 98308
  8.6 125.5 %all-to-all-start = ((bf16[1,1,128,2,128,20]{2,3,5,1,0,4:T(2,128)(2,1)}), bf16[1,1,128,2,128,20]{2,3,5,1,0,4:T(2,128)(2,1)S(1)}, u32[]{:S(2)}, u32[]{:S(2)}) async-start(bf16[1,1,128,2,128,20]{2,3,5,1,0,4:T(2,128)(2,1)} %copy.49), calls=%async_computation | async-start | bytes 2621440 | tf_op jit(solution)/shard_map/all_to_all | solution.py:110
  234.6 60.2 %copy-start.2 = (f32[1,1024,2,128]{1,3,2,0:T(8,128)S(1)}, f32[1,1024,2,128]{1,3,2,0:T(8,128)}, u32[]{:S(2)}) copy-start(f32[1,1024,2,128]{1,3,2,0:T(8,128)} %get-tuple-element.7) | copy-start | bytes 3145732
  234.6 60.2 %copy-start.3 = (f32[1,1024,2,128]{1,3,2,0:T(8,128)S(1)}, f32[1,1024,2,128]{1,3,2,0:T(8,128)}, u32[]{:S(2)}) copy-start(f32[1,1024,2,128]{1,3,2,0:T(8,128)} %get-tuple-element.8) | copy-start | bytes 3145732
  234.6 94.3 %copy-start.4 = (bf16[20,128]{1,0:T(8,128)(2,1)S(1)}, bf16[20,128]{1,0:T(8,128)(2,1)}, u32[]{:S(2)}) copy-start(bf16[20,128]{1,0:T(8,128)(2,1)} %param.12) | copy-start | bytes 15364
  321.7 98.3 %all-to-all-start.1 = ((bf16[1,1,1024,2,16,128]{5,3,4,1,0,2:T(2,128)(2,1)}), bf16[1,1,1024,2,16,128]{5,3,4,1,0,2:T(2,128)(2,1)}, u32[]{:S(2)}, u32[]{:S(2)}) async-start(bf16[1,1,1024,2,16,128]{5,3,4,1,0,2:T(2,128)(2,1)} %copy.65), calls=%async_computation.1 | async-start | bytes 16777216 | tf_op jit(solution)/shard_map/all_to_all | solution.py:138
  356.2 99.6 %copy-start.5 = (bf16[128,128]{1,0:T(8,128)(2,1)S(1)}, bf16[128,128]{1,0:T(8,128)(2,1)}, u32[]{:S(2)}) copy-start(bf16[128,128]{1,0:T(8,128)(2,1)} %param.18) | copy-start | bytes 98308
  356.2 99.6 %copy-start.6 = (bf16[128,20]{0,1:T(8,128)(2,1)S(1)}, bf16[128,20]{0,1:T(8,128)(2,1)}, u32[]{:S(2)}) copy-start(bf16[128,20]{0,1:T(8,128)(2,1)} %param.20) | copy-start | bytes 15364
  356.2 99.6 %copy-start.7 = (f32[20]{0:T(128)S(1)}, f32[20]{0:T(128)}, u32[]{:S(2)}) copy-start(f32[20]{0:T(128)} %param.21) | copy-start | bytes 244
  356.2 99.6 %copy-start.8 = (f32[128]{0:T(128)S(1)}, f32[128]{0:T(128)}, u32[]{:S(2)}) copy-start(f32[128]{0:T(128)} %param.19) | copy-start | bytes 1540
  356.2 99.6 %copy-start.9 = (f32[128]{0:T(128)S(1)}, f32[128]{0:T(128)}, u32[]{:S(2)}) copy-start(f32[128]{0:T(128)} %param.13) | copy-start | bytes 1540
  455.8 175.9 %copy-start.1 = (bf16[16,32,32]{2,1,0:T(8,128)(2,1)S(1)}, bf16[16,32,32]{2,1,0:T(8,128)(2,1)}, u32[]{:S(2)}) copy-start(bf16[16,32,32]{2,1,0:T(8,128)(2,1)} %param.15) | copy-start | bytes 98308
where the time goes:
time: 640 us; the launch traced here: 632 us
  matrix products  291 us (45%)
  local copies, waits for them, and re-layouts  170 us (27%)
  blocking collectives  83.9 us (13%)
  waiting for transfers between devices  63.8 us (10%)
  other arithmetic  12.5 us (2%)
  starting transfers between devices  10.3 us (2%)
    dot_general x1, matrix products, shards(): jnp.einsum('fxyc,cv->fvxy', active, out_weight, preferred_element_type=jn...  168 us
    all_to_all x1, waiting for transfers between devices, shards(): lax.all_to_all(col_modes, ('mode', 'cores'), split_axis=2, concat_axis=4,...  63.7 us
    convert_element_type x1, local copies, waits for them, and re-layouts, shards(): projected = jnp.einsum('fqkmc,cbe->fqkmbe', spectrum, input_whole, prefer...  54.9 us
    another operation x2, local copies, waits for them, and re-layouts  48.3 us
    all_gather x1, blocking collectives, shards(): lax.all_gather(output_core, 'batch', axis=0, tiled=True)  36.8 us
    dot_general x1, matrix products, shards(): jnp.einsum('kmab,fqkmbe->fqkmae', mode_factor, projected, preferred_eleme...  28.3 us
    dot_general x1, matrix products, shards(): jnp.einsum('fvxy,vc->fxyc', fields, lift_weight, preferred_element_type=j...  27.3 us
    dot_general x1, matrix products, shards(): jnp.einsum('fxpmc,pmy->fxyc', returned[:, 0], width_back, preferred_eleme...  26.7 us
  transfers between devices with their start and end apart: 2, of which 1 were waited for; matrix products, arithmetic and copies ran while one was open for 10% of the time, Pallas kernels for 0%

commit v1 on v0

--- a/solution.py
+++ b/solution.py
@@ -2,7 +2,11 @@
 
 import jax
 import jax.numpy as jnp
+import ml_dtypes
+import numpy as np
 from jax import lax
+from jax.experimental import pallas as pl
+from jax.experimental.pallas import tpu as pltpu
 from jax.sharding import PartitionSpec as P
 
 NX = 1024
@@ -150,6 +154,311 @@
     return result.astype(jnp.bfloat16)
 
 
+def cyclic_rows(row_count, holders):
+    return (np.arange(row_count)[None, :] * holders + np.arange(holders)[:, None]).reshape(-1)
+
+
+def host_pair(waves, points, length):
+    steps = np.asarray(waves)[:, None] * np.asarray(points)[None, :] % length
+    angles = steps.astype(np.float32) * np.float32(TWO_PI / length)
+    return np.cos(angles), np.sin(angles)
+
+
+def dense(a, b, contract=((1,), (0,))):
+    return lax.dot_general(a, b, (contract, ((), ())), preferred_element_type=jnp.float32)
+
+
+GROUP = 4
+PACK = 16
+
+
+def mix_kernel(
+    arrived, height, lift, row_sum, bias_row, joined, first, back, spread,
+    mixed, stacked, spectrum, blocks, closing, weights, parts, carried,
+):
+    group = pl.program_id(0)
+    holders, lead, _ = arrived.shape
+    waves = lead // 2
+    rank = first.shape[1]
+    variables = stacked.shape[0] // waves
+    row_count = arrived.shape[2] // variables
+    kx_count = mixed.shape[0] // 2
+    channels = joined.shape[1]
+    packs = kx_count // PACK
+    groups = waves // GROUP
+    span = rank * PACK
+    wide = GROUP * rank
+
+    @pl.when(group == 0)
+    def _():
+        for d in range(holders):
+            for p in range(2):
+                for v in range(variables):
+                    stacked[v * waves:(v + 1) * waves, (d * 2 + p) * row_count:(d * 2 + p + 1) * row_count] = (
+                        arrived[d, p * waves:(p + 1) * waves, v * row_count:(v + 1) * row_count]
+                    )
+        by_variable = dense(height[...], stacked[...], ((1,), (1,))).astype(jnp.bfloat16)
+        for g in range(groups):
+            lanes = slice(g * GROUP * channels, (g + 1) * GROUP * channels)
+            spectrum[g] = (
+                dense(by_variable, lift[:, lanes]) + row_sum[...] * bias_row[:, lanes]
+            ).astype(jnp.bfloat16)
+        down = lax.broadcasted_iota(jnp.int32, (span, span), 0) % PACK
+        across = lax.broadcasted_iota(jnp.int32, (span, span), 1) % PACK
+        same = down == across
+        for k in range(packs):
+            full = dense(first[k * span:(k + 1) * span, :], spread[...])
+            blocks[k] = jnp.where(same, full, 0.0).astype(jnp.bfloat16)
+        closing[...] = jnp.zeros_like(closing)
+        outs = back.shape[1]
+        for a in range(rank):
+            for m in range(GROUP):
+                closing[(a * GROUP + m) * rank:(a * GROUP + m + 1) * rank, m * outs:(m + 1) * outs] = (
+                    back[a * rank:(a + 1) * rank, :]
+                )
+
+    own = spectrum[group]
+    owner = lax.broadcasted_iota(jnp.int32, (channels, wide), 1) // rank
+    for part in range(rank // 8):
+        for b in range(8):
+            block = joined[part * 8 + b]
+            for m in range(GROUP):
+                weights[m * channels:(m + 1) * channels, b * wide:(b + 1) * wide] = jnp.where(
+                    owner == m, block, jnp.zeros_like(block)
+                )
+        got = dense(own, weights[...]).astype(jnp.bfloat16)
+        for b in range(8):
+            for q in range(2):
+                parts[part * 8 + b, :, q * wide:(q + 1) * wide] = got[
+                    q * kx_count:(q + 1) * kx_count, b * wide:(b + 1) * wide
+                ]
+    for k in range(packs):
+        rows = parts[:, k * PACK:(k + 1) * PACK, :].reshape(span, 2 * wide)
+        got = dense(blocks[k], rows).astype(jnp.bfloat16)
+        for a in range(rank):
+            for q in range(2):
+                carried[q * kx_count + k * PACK:q * kx_count + (k + 1) * PACK, a * wide:(a + 1) * wide] = got[
+                    a * PACK:(a + 1) * PACK, q * wide:(q + 1) * wide
+                ]
+    traced = dense(carried[...], closing[...])
+    outs = back.shape[1]
+    for m in range(GROUP):
+        one = traced[:, m * outs:(m + 1) * outs]
+        real = one[:kx_count, :channels] - one[kx_count:, channels:]
+        imaginary = one[:kx_count, channels:] + one[kx_count:, :channels]
+        mixed[:kx_count, m * channels:(m + 1) * channels] = real.astype(jnp.bfloat16)
+        mixed[kx_count:, m * channels:(m + 1) * channels] = imaginary.astype(jnp.bfloat16)
+
+
+def mix(arrived, height, lift, row_sum, bias_row, joined, first, back, spread):
+    holders, lead, flat = arrived.shape
+    waves = lead // 2
+    variables = lift.shape[0] // waves
+    rank, channels, _ = joined.shape
+    kx2 = height.shape[0]
+    kx_count = kx2 // 2
+    groups = waves // GROUP
+    span = rank * PACK
+    wide = GROUP * rank
+
+    def whole(a):
+        return pl.BlockSpec(a.shape, lambda g: (0,) * a.ndim)
+
+    return pl.pallas_call(
+        mix_kernel,
+        grid=(groups,),
+        in_specs=[
+            whole(arrived), whole(height), whole(lift), whole(row_sum), whole(bias_row),
+            pl.BlockSpec((rank, channels, wide), lambda g: (0, 0, g)),
+            whole(first), whole(back), whole(spread),
+        ],
+        out_specs=pl.BlockSpec((kx2, GROUP * channels), lambda g: (0, g)),
+        out_shape=jax.ShapeDtypeStruct((kx2, waves * channels), jnp.bfloat16),
+        scratch_shapes=[
+            pltpu.VMEM((variables * waves, height.shape[1]), jnp.bfloat16),
+            pltpu.VMEM((groups, kx2, GROUP * channels), jnp.bfloat16),
+            pltpu.VMEM((kx_count // PACK, span, span), jnp.bfloat16),
+            pltpu.VMEM((rank * wide, GROUP * back.shape[1]), jnp.bfloat16),
+            pltpu.VMEM((GROUP * channels, 8 * wide), jnp.bfloat16),
+            pltpu.VMEM((rank, kx_count, 2 * wide), jnp.bfloat16),
+            pltpu.VMEM((kx2, rank * wide), jnp.bfloat16),
+        ],
+        compiler_params=pltpu.CompilerParams(vmem_limit_bytes=48 * 2**20),
+        name="mix",
+    )(arrived, height, lift, row_sum, bias_row, joined, first, back, spread)
+
+
+def rows_kernel(table, gathered, cols, turned):
+    row_count, waves, channels = turned.shape
+    for p in range(2):
+        got = dense(table[p * row_count:(p + 1) * row_count, :], gathered[0])
+        for m in range(waves):
+            turned[:, m, :] = got[:, m * channels:(m + 1) * channels]
+        cols[:, p] = turned[...].astype(jnp.bfloat16)
+
+
+def rows_back(table, gathered, waves):
+    holders, kx2, flat = gathered.shape
+    row_count = table.shape[0] // 2
+    channels = flat // waves
+    return pl.pallas_call(
+        rows_kernel,
+        grid=(holders,),
+        in_specs=[
+            pl.BlockSpec(table.shape, lambda d: (0, 0)),
+            pl.BlockSpec((1, kx2, flat), lambda d: (d, 0, 0)),
+        ],
+        out_specs=pl.BlockSpec((row_count, 2, waves, channels), lambda d: (0, 0, d, 0)),
+        out_shape=jax.ShapeDtypeStruct((row_count, 2, holders * waves, channels), jnp.bfloat16),
+        scratch_shapes=[pltpu.VMEM((row_count, waves, channels), jnp.float32)],
+        compiler_params=pltpu.CompilerParams(vmem_limit_bytes=48 * 2**20),
+        name="rows_back",
+    )(table, gathered)
+
+
+LANES = 256
+
+
+def gelu(h):
+    return h * (0.5 + 0.5 * lax.erf(h * (1.0 / math.sqrt(2.0))))
+
+
+def finish_kernel(fields, cols, width, skip, bias, closing, out_bias, result, turned, active):
+    variables, rows, points = fields.shape
+    channels = cols.shape[2]
+    for x in range(rows):
+        turned[x * channels:(x + 1) * channels, :] = cols[x].T
+
+    def step(i, carry):
+        start = pl.multiple_of(i * LANES, LANES)
+        lanes = pl.ds(start, LANES)
+        source = fields[:, :, lanes].reshape(variables * rows, LANES)
+        table = width[:, lanes]
+        depth = 2 * channels
+        for x in range(rows // 2):
+            here = slice(x * depth, (x + 1) * depth)
+            total = dense(turned[here, :], table) + dense(skip[here, :], source) + bias[here, :]
+            active[here, :] = gelu(total).astype(jnp.bfloat16)
+        got = dense(closing[...], active[...]) + out_bias[...]
+        result[:, :, lanes] = got.astype(jnp.bfloat16).reshape(variables, rows, LANES)
+        return carry
+
+    lax.fori_loop(0, points // LANES, step, 0)
+
+
+def finish(fields, cols, width, skip, bias, closing, out_bias):
+    variables, row_count, points = fields.shape
+    depth, channels = cols.shape[1:]
+
+    def whole(a):
+        return pl.BlockSpec(a.shape, lambda i: (0,) * a.ndim)
+
+    return pl.pallas_call(
+        finish_kernel,
+        grid=(row_count // PACK,),
+        in_specs=[
+            pl.BlockSpec((variables, PACK, points), lambda i: (0, i, 0)),
+            pl.BlockSpec((PACK, depth, channels), lambda i: (i, 0, 0)),
+            whole(width), whole(skip), whole(bias), whole(closing), whole(out_bias),
+        ],
+        out_specs=pl.BlockSpec((variables, PACK, points), lambda i: (0, i, 0)),
+        out_shape=jax.ShapeDtypeStruct(fields.shape, jnp.bfloat16),
+        scratch_shapes=[
+            pltpu.VMEM((PACK * channels, depth), jnp.bfloat16),
+            pltpu.VMEM((PACK * channels, LANES), jnp.bfloat16),
+        ],
+        compiler_params=pltpu.CompilerParams(vmem_limit_bytes=48 * 2**20),
+        name="finish",
+    )(fields, cols, width, skip, bias, closing, out_bias)
+
+
+def gather_factors(first_core, input_core, output_core):
+    count, rank, _ = first_core.shape
+    flat = jnp.concatenate(
+        [first_core.reshape(-1), input_core.reshape(-1), output_core.reshape(-1)]
+    ).reshape(-1, 128)
+    whole = lax.all_gather(flat, "batch", axis=0, tiled=False)
+    parts = whole.shape[0]
+    size = first_core.size
+    whole = whole.reshape(parts, -1)
+    first = whole[:, :size].reshape(parts * count, rank, rank)
+    inner = whole[:, size:2 * size].reshape(parts * count, rank, rank)
+    outer = whole[:, 2 * size:].reshape(parts * count, 2, rank, rank)
+    return first, inner, outer
+
+
+def fast_shards(
+    fields, lift_weight, lift_bias, first_core, second_core, input_core, output_core,
+    skip_weight, skip_bias, out_weight, out_bias,
+):
+    holders = lax.axis_size("mode") * lax.axis_size("cores")
+    waves, rank, _ = second_core.shape
+    _, variables, row_count, points = fields.shape
+    channels = lift_weight.shape[1]
+    fields = fields[0]
+    me = lax.axis_index("mode") * lax.axis_size("cores") + lax.axis_index("cores")
+
+    cosines, sines = host_pair(np.arange(MY), np.arange(points), points)
+    root = math.sqrt(points)
+    forward = np.stack([cosines, -sines], 0).reshape(2, holders, waves, points).transpose(1, 0, 2, 3)
+    forward = jnp.asarray((forward.reshape(2 * MY, points) / root).astype(np.float32)).astype(jnp.bfloat16)
+    weight = np.where(np.arange(MY) == 0, 1.0, 2.0).astype(np.float32)[:, None]
+    width = np.concatenate([cosines * weight, -sines * weight], 0) / root
+    width = jnp.asarray(width.astype(ml_dtypes.bfloat16))
+    order = cyclic_rows(row_count, holders)
+    root = math.sqrt(NX)
+    cosines, sines = host_pair(np.arange(MX) - MX // 2, order, NX)
+    cosines, sines = [t.reshape(MX, holders, row_count) / root for t in (cosines, sines)]
+    upper = np.stack([cosines, sines], 2)
+    lower = np.stack([-sines, cosines], 2)
+    height = np.stack([upper, lower], 0).reshape(2 * MX, -1).astype(ml_dtypes.bfloat16)
+    real_part = np.asarray(height, np.float32).reshape(2 * MX, holders, 2, row_count)[:, :, 0]
+    row_sum = real_part.sum((1, 2), dtype=np.float64).astype(np.float32)[:, None]
+    cos_t, sin_t = [t.transpose(1, 2, 0) for t in (cosines, sines)]
+    up = np.concatenate([cos_t, -sin_t], 2)
+    low = np.concatenate([sin_t, cos_t], 2)
+    back_rows = jnp.asarray(np.concatenate([up, low], 1).astype(ml_dtypes.bfloat16))
+    back_rows = lax.dynamic_index_in_dim(back_rows, me, 0, keepdims=False)
+
+    first, inner, outer = gather_factors(first_core, input_core, output_core)
+    modes = jnp.einsum(
+        "ry,vxy->rvx", forward, fields, preferred_element_type=jnp.float32
+    ).astype(jnp.bfloat16)
+    modes = modes.reshape(holders, 2 * waves, variables * row_count)
+    arrived = lax.all_to_all(modes, ("mode", "cores"), split_axis=0, concat_axis=0, tiled=True)
+
+    same = jnp.eye(waves, dtype=jnp.bfloat16)
+    lift = (lift_weight[:, None, None, :] * same[None, :, :, None]).reshape(
+        variables * waves, waves * channels
+    )
+    is_zero = (me * waves + jnp.arange(waves) == 0).astype(jnp.float32)
+    bias_value = (math.sqrt(points) * lift_bias).astype(jnp.bfloat16).astype(jnp.float32)
+    bias_row = (is_zero[:, None] * bias_value[None, :]).reshape(1, -1)
+    joined = jnp.einsum(
+        "mbd,cde->bcme", second_core, inner, preferred_element_type=jnp.float32
+    ).astype(jnp.bfloat16).reshape(rank, channels, waves * rank)
+    packed = first.reshape(MX // PACK, PACK, rank, rank).transpose(0, 2, 1, 3).reshape(-1, rank)
+    back = outer.transpose(3, 2, 1, 0).reshape(rank * rank, -1)
+    spread = jnp.asarray(np.repeat(np.eye(rank), PACK, axis=1).astype(ml_dtypes.bfloat16))
+    mixed = mix(
+        arrived, jnp.asarray(height), lift, jnp.asarray(row_sum), bias_row, joined, packed, back, spread
+    )
+    gathered = lax.all_gather(mixed, ("mode", "cores"), axis=0, tiled=False)
+    cols = rows_back(back_rows, gathered, waves).reshape(row_count, 2 * MY, channels)
+
+    skip_wide = skip_weight.astype(jnp.float32)
+    direct = jnp.dot(lift_weight.astype(jnp.float32), skip_wide, precision="highest")
+    total_bias = jnp.dot(lift_bias, skip_wide, precision="highest") + skip_bias
+    rows_eye = jnp.eye(PACK, dtype=jnp.float32)
+    skip = (rows_eye[:, None, None, :] * direct.T[None, :, :, None]).astype(jnp.bfloat16)
+    skip = skip.reshape(PACK * channels, variables * PACK)
+    closing = out_weight.T[:, None, None, :] * rows_eye.astype(jnp.bfloat16)[None, :, :, None]
+    closing = closing.reshape(variables * PACK, PACK * channels)
+    bias = jnp.tile(total_bias, PACK)[:, None]
+    last_bias = jnp.repeat(out_bias, PACK)[:, None]
+    return finish(fields, cols, width, skip, bias, closing, last_bias)[None]
+
+
 def solution(mesh):
     placed = (
         P("batch", None, ("mode", "cores"), None),
@@ -164,8 +473,10 @@
         P(),
         P(),
     )
+    holders = mesh.shape["mode"] * mesh.shape["cores"]
+    fits = MY // holders % PACK == 0 and NX // holders % 128 == 0
     return jax.shard_map(
-        shards,
+        fast_shards if fits else shards,
         mesh=mesh,
         in_specs=placed,
         out_specs=P("batch", None, ("mode", "cores"), None),

time: 640 us -> 222 us (0.35); the launches traced: 632 us -> 221 us
  matrix products: 291 us -> 5.51 us
  local copies, waits for them, and re-layouts: 170 us -> 40.9 us
  Pallas kernels: 0 us -> 88.9 us
  blocking collectives: 83.9 us -> 0 us
  between operations: 0.66 us -> 13.7 us
  other arithmetic: 12.5 us -> 1.54 us
    dot_general x10 -> x4, matrix products: 291 us -> 5.51 us  [the longest x1 4.04 us: fast_shards(): jnp.einsum('ry,vxy->rvx', forward, fields, preferred_element_type=jnp.flo...]
    convert_element_type x4 -> x5, local copies, waits for them, and re-layouts: 107 us -> 6.83 us  [the longest x1 4.71 us: fast_shards(): joined = jnp.einsum('mbd,cde->bcme', second_core, inner, preferred_elemen...]
    pallas_call x0 -> x3, Pallas kernels: none -> 88.9 us  [the longest x1 47.7 us: finish(): pl.pallas_call(finish_kernel, grid=(row_count // PACK,), in_specs=[pl.Blo...]
    all_gather x3 -> x0, blocking collectives: 83.9 us -> none  [the longest x1 36.8 us: shards(): lax.all_gather(output_core, 'batch', axis=0, tiled=True)]
    all_gather x0 -> x2, waiting for transfers between devices: none -> 65.5 us  [the longest x1 48.5 us: fast_shards(): gathered = lax.all_gather(mixed, ('mode', 'cores'), axis=0, tiled=False)]
    all_to_all x2 -> x1, waiting for transfers between devices: 63.8 us -> 0.01 us  [fast_shards(): lax.all_to_all(modes, ('mode', 'cores'), split_axis=0, concat_axis=0, til...]
    another operation x3 -> x4, local copies, waits for them, and re-layouts: 48.3 us -> 2.11 us  [the longest x2 1.41 us: fast_shards(): bias = jnp.tile(total_bias, PACK)[:, None]]
    reshape x0 -> x8, local copies, waits for them, and re-layouts: none -> 17.4 us  [the longest x1 6.51 us: fast_shards(): joined = jnp.einsum('mbd,cde->bcme', second_core, inner, preferred_elemen...]
  transfers between devices with their start and end apart: 2 -> 3, of which waited for: 1 -> 2; matrix products, arithmetic and copies ran while one was open for 10% -> 19% of each run, Pallas kernels for 0% -> 0%
where the time goes in v1:
time: 222 us; the launch traced here: 221 us
  Pallas kernels  88.9 us (40%)
  waiting for transfers between devices  65.5 us (30%)
  local copies, waits for them, and re-layouts  40.9 us (18%)
  between operations  13.7 us (6%)
  matrix products  5.51 us (2%)
  starting transfers between devices  5.34 us (2%)
    all_gather x1, waiting for transfers between devices, fast_shards(): gathered = lax.all_gather(mixed, ('mode', 'cores'), axis=0, tiled=False)  48.5 us
    pallas_call x1, Pallas kernels, finish(): pl.pallas_call(finish_kernel, grid=(row_count // PACK,), in_specs=[pl.Blo...  47.7 us
    pallas_call x1, Pallas kernels, mix(): pl.pallas_call(mix_kernel, grid=(groups,), in_specs=[whole(arrived), whol...  26.1 us
    all_gather x1, waiting for transfers between devices, gather_factors(): whole = lax.all_gather(flat, 'batch', axis=0, tiled=False)  17 us
    pallas_call x1, Pallas kernels, rows_back(): pl.pallas_call(rows_kernel, grid=(holders,), in_specs=[pl.BlockSpec(table...  15.1 us
    unnamed x37, local copies, waits for them, and re-layouts  6.83 us
    reshape x1, local copies, waits for them, and re-layouts, fast_shards(): joined = jnp.einsum('mbd,cde->bcme', second_core, inner, preferred_elemen...  6.51 us
    all_to_all x1, starting transfers between devices, fast_shards(): lax.all_to_all(modes, ('mode', 'cores'), split_axis=0, concat_axis=0, til...  5.3 us
  transfers between devices with their start and end apart: 3, of which 2 were waited for; matrix products, arithmetic and copies ran while one was open for 19% of the time, Pallas kernels for 0%

profile of v1, /device:TPU:0, one launch (start us, length us, event | category | flops | bytes accessed | tf_op | source)
XLA Modules:
  0.0 221.4 jit_solution(10638894772983017885)
XLA Ops:
  6.5 1.5 reshape.105
  8.0 1.2 reshape.103
  9.2 1.2 reshape.104
  10.3 0.7 maximum_bitcast_fusion
  11.1 4.0 %convolution_convert_fusion = bf16[256,20,128]{2,0,1:T(8,128)(2,1)S(1)} fusion(bf16[256,1024,1]{1,0,2:T(8,128)(2,1)S(1)} %copy-done.15, bf16[1,20,128,1024]{3,2,1,0:T(8,128)(2,1)} %param.17), kind=kOutput, calls=%fused_computation.2 | convolution fusion | flops 1342832640 | bytes 7077888 | tf_op jit(solution)/shard_map/ry,vxy->rvx/dot_general | solution.py:424
  15.1 0.9 copy.32
  16.0 1.7 reshape.102
  17.7 5.3 %all-to-all-start = ((bf16[8,32,2560]{2,1,0:T(8,128)(2,1)}), bf16[8,32,2560]{2,1,0:T(8,128)(2,1)S(1)}, u32[]{:S(2)}, u32[]{:S(2)}) async-start(bf16[8,32,2560]{2,1,0:T(8,128)(2,1)} %reshape.102), calls=%async_computation | async-start | bytes 2621440 | tf_op jit(solution)/shard_map/all_to_all | solution.py:428
  23.3 1.4 copy.58
  24.8 17.0 %all-gather.4.cloned.1.call-done = bf16[4,1024,128]{2,1,0:T(8,128)(2,1)} async-done(((bf16[1,1024,128]{2,1,0:T(8,128)(2,1)}), bf16[4,1024,128]{2,1,0:T(8,128)(2,1)}) %all-gather.4.cloned.1.call-update) | async-done | bytes 1048592 | tf_op jit(solution)/shard_map/all_gather | solution.py:380
  41.9 2.0 copy.59
  43.9 0.9 fusion.7
  44.8 1.0 slice.14
  45.7 0.6 reshape.107
  46.3 1.3 copy.43
  47.7 1.2 convert_bitcast_fusion
  48.9 4.7 %copy.35 = bf16[32,128,16,32]{1,3,2,0:T(8,128)(2,1)} copy(bf16[32,128,16,32]{1,0,2,3:T(8,128)(2,1)S(1)} %convert_bitcast_fusion) | data formatting | bytes 8388608 | tf_op jit(solution)/shard_map/convert_element_type | solution.py:439
  53.6 6.5 %copy.38.joined = bf16[32,128,512]{2,1,0:T(8,128)(2,1)} copy(bf16[32,128,512]{1,2,0:T(8,128)(2,1)} %bitcast.69) | data formatting | bytes 8388608 | tf_op jit(solution)/shard_map/reshape | solution.py:439
  60.1 0.6 reshape_reshape.3
  60.7 0.4 copy.36
  61.1 3.6 %reshape.110 = bf16[128,2,32,32]{3,2,1,0:T(8,128)(2,1)} reshape(bf16[4,65536]{1,0:T(4,128)(2,1)} %slice.14) | data formatting | bytes 1048576 | tf_op jit(solution)/shard_map/reshape | solution.py:386
  64.7 4.5 %copy.37 = bf16[32,32,2,128]{3,2,1,0:T(2,128)(2,1)} copy(bf16[32,32,2,128]{0,1,2,3:T(8,128)(2,1)} %bitcast.70) | data formatting | bytes 1048576 | tf_op jit(solution)/shard_map/transpose | solution.py:441
  69.2 1.1 copy.60
  70.4 1.2 copy-done.3
  71.6 26.1 %mix.1 = bf16[256,2048]{1,0:T(8,128)(2,1)} custom-call(bf16[8,32,2560]{2,1,0:T(8,128)(2,1)S(1)} %all-to-all-done.arrived, bf16[256,2048]{1,0:T(8,128)(2,1)S(1)} %copy-done.3, bf16[320,2048]{1,0:T(8,128)(2,1)} %bitcast.72, f32[256,1]{1,0:T(8,128)S(1)} %copy-done.5, f32[1,2048]{1,0:T(1,128)S(1)} %bitcast.67, bf16[32,128,512]{2,1,0:T(8,128)(2,1)} %copy.38.joined, ...), custom_call_target="tpu_custom_call" | custom-call | tf_op jit(solution)/shard_map/mix/pallas_call | solution.py:267
  97.8 0.4 multiply_convert_fusion
  98.6 1.1 copy.40.skip
  100.7 1.4 copy.41.bias
  102.3 0.9 dynamic-slice_bitcast_fusion.table
  103.3 48.5 %all-gather.6.cloned.1.call-done = bf16[2048,2048]{1,0:T(8,128)(2,1)} async-done(((bf16[256,2048]{1,0:T(8,128)(2,1)}), bf16[2048,2048]{1,0:T(8,128)(2,1)}) %all-gather.6.cloned.1.call-update) | async-done | bytes 8388624 | tf_op jit(solution)/shard_map/all_gather | solution.py:446
  151.7 15.1 %rows_back.1 = bf16[128,2,128,128]{3,2,1,0:T(8,128)(2,1)} custom-call(bf16[256,256]{1,0:T(8,128)(2,1)S(1)} %dynamic-slice_bitcast_fusion.table, bf16[8,256,2048]{2,1,0:T(8,128)(2,1)} %bitcast.71), custom_call_target="tpu_custom_call" | custom-call | tf_op jit(solution)/shard_map/rows_back/pallas_call | solution.py:304
  166.8 47.7 %finish.1 = bf16[20,128,1024]{2,1,0:T(8,128)(2,1)} custom-call(bf16[20,128,1024]{2,1,0:T(8,128)(2,1)} %bitcast.77, bf16[128,256,128]{2,1,0:T(8,128)(2,1)} %bitcast.68, bf16[256,1024]{1,0:T(8,128)(2,1)S(1)} %copy-done.4, bf16[2048,320]{1,0:T(8,128)(2,1)S(1)} %copy.40.skip, f32[2048,1]{1,0:T(8,128)S(1)} %copy-done.2, bf16[320,2048]{1,0:T(8,128)(2,1)S(1)} %bitcast.64, ...), custom_call_target="tpu_custom_call" | custom-call | tf_op jit(solution)/shard_map/finish/pallas_call | solution.py:356
  (53 shorter events, 2.2 us)
Async XLA Ops:
  6.5 41.1 %copy-start = (bf16[16,32,32]{2,1,0:T(8,128)(2,1)S(1)}, bf16[16,32,32]{2,1,0:T(8,128)(2,1)}, u32[]{:S(2)}) copy-start(bf16[16,32,32]{2,1,0:T(8,128)(2,1)} %param.21) | copy-start | bytes 98308
  6.5 4.5 %copy-start.15 = (bf16[256,1024,1]{1,0,2:T(8,128)(2,1)S(1)}, bf16[256,1024,1]{1,0,2:T(8,128)(2,1)}, u32[]{:S(2)}) copy-start(bf16[256,1024,1]{1,0,2:T(8,128)(2,1)} %constant.42) | copy-start | bytes 1572868
  6.5 35.3 %all-gather.4.cloned.1.call-start = ((), (), s32[]{:S(2)}) async-start(), calls=%async_computation.1 | async-start | bytes 1310720 | tf_op jit(solution)/shard_map/all_gather | solution.py:380
  17.7 5.5 %copy-start.9 = (bf16[20,128]{1,0:T(8,128)(2,1)S(1)}, bf16[20,128]{1,0:T(8,128)(2,1)}, u32[]{:S(2)}) copy-start(bf16[20,128]{1,0:T(8,128)(2,1)} %param.18) | copy-start | bytes 15364
  17.7 52.6 %all-to-all-start = ((bf16[8,32,2560]{2,1,0:T(8,128)(2,1)}), bf16[8,32,2560]{2,1,0:T(8,128)(2,1)S(1)}, u32[]{:S(2)}, u32[]{:S(2)}) async-start(bf16[8,32,2560]{2,1,0:T(8,128)(2,1)} %reshape.102), calls=%async_computation | async-start | bytes 2621440 | tf_op jit(solution)/shard_map/all_to_all | solution.py:428
  23.0 128.7 %all-gather.6.cloned.1.call-start = ((), (), s32[]{:S(2)}) async-start(), calls=%async_computation.2 | async-start | bytes 9437184 | tf_op jit(solution)/shard_map/all_gather | solution.py:446
  23.3 1.4 copy-start.12
  53.6 6.5 %copy-start.7 = (bf16[4,32768]{1,0:T(4,128)(2,1)S(1)}, bf16[4,32768]{1,0:T(4,128)(2,1)}, u32[]{:S(2)}) copy-start(bf16[4,32768]{1,0:T(4,128)(2,1)} %get-tuple-element.5) | copy-start | bytes 786436
  64.7 5.6 %copy-start.5 = (f32[256,1]{1,0:T(8,128)S(1)}, f32[256,1]{1,0:T(8,128)}, u32[]{:S(2)}) copy-start(f32[256,1]{1,0:T(8,128)} %constant.39.clone.row_sum) | copy-start | bytes 3076
  64.7 5.6 %copy-start.6 = (bf16[32,512]{1,0:T(8,128)(2,1)S(1)}, bf16[32,512]{1,0:T(8,128)(2,1)}, u32[]{:S(2)}) copy-start(bf16[32,512]{1,0:T(8,128)(2,1)} %constant.37.clone.spread) | copy-start | bytes 98308
  70.4 1.2 copy-start.3
  71.6 26.1 %copy-start.8 = (bf16[128,128]{1,0:T(8,128)(2,1)S(1)}, bf16[128,128]{1,0:T(8,128)(2,1)}, u32[]{:S(2)}) copy-start(bf16[128,128]{1,0:T(8,128)(2,1)} %param.24) | copy-start | bytes 98308
  98.5 1.2 copy-start.10
  99.9 0.7 copy-start.13
  99.9 0.7 copy-start.14
  100.0 2.2 copy-start.11
  151.7 15.1 %copy-start.2 = (f32[2048,1]{1,0:T(8,128)S(1)}, f32[2048,1]{1,0:T(8,128)}, u32[]{:S(2)}) copy-start(f32[2048,1]{1,0:T(8,128)} %copy.41.bias) | copy-start | bytes 24580
  151.7 15.1 %copy-start.4 = (bf16[256,1024]{1,0:T(8,128)(2,1)S(1)}, bf16[256,1024]{1,0:T(8,128)(2,1)}, u32[]{:S(2)}) copy-start(bf16[256,1024]{1,0:T(8,128)(2,1)} %constant.35.clone.width) | copy-start | bytes 1572868
  166.8 47.7 %copy-start.1 = (bf16[16,32,32]{2,1,0:T(8,128)(2,1)S(1)}, bf16[16,32,32]{2,1,0:T(8,128)(2,1)}, u32[]{:S(2)}) copy-start(bf16[16,32,32]{2,1,0:T(8,128)(2,1)} %param.21) | copy-start | bytes 98308
Sparse Core Ops, SparseCore 0:
  11.2 30.6 all-gather.3
  97.8 53.8 all-gather.5

commit v2 on v1

--- a/solution.py
+++ b/solution.py
@@ -1,3 +1,4 @@
+import functools
 import math
 
 import jax
@@ -173,7 +174,7 @@
 
 
 def mix_kernel(
-    arrived, height, lift, row_sum, bias_row, joined, first, back, spread,
+    base, arrived, height, lift, row_sum, bias_row, joined, first, back, spread,
     mixed, stacked, spectrum, blocks, closing, weights, parts, carried,
 ):
     group = pl.program_id(0)
@@ -185,7 +186,7 @@
     kx_count = mixed.shape[0] // 2
     channels = joined.shape[1]
     packs = kx_count // PACK
-    groups = waves // GROUP
+    groups = spectrum.shape[0]
     span = rank * PACK
     wide = GROUP * rank
 
@@ -199,7 +200,7 @@
                     )
         by_variable = dense(height[...], stacked[...], ((1,), (1,))).astype(jnp.bfloat16)
         for g in range(groups):
-            lanes = slice(g * GROUP * channels, (g + 1) * GROUP * channels)
+            lanes = slice((base + g) * GROUP * channels, (base + g + 1) * GROUP * channels)
             spectrum[g] = (
                 dense(by_variable, lift[:, lanes]) + row_sum[...] * bias_row[:, lanes]
             ).astype(jnp.bfloat16)
@@ -250,14 +251,13 @@
         mixed[kx_count:, m * channels:(m + 1) * channels] = imaginary.astype(jnp.bfloat16)
 
 
-def mix(arrived, height, lift, row_sum, bias_row, joined, first, back, spread):
+def mix(base, groups, arrived, height, lift, row_sum, bias_row, joined, first, back, spread):
     holders, lead, flat = arrived.shape
     waves = lead // 2
     variables = lift.shape[0] // waves
     rank, channels, _ = joined.shape
     kx2 = height.shape[0]
     kx_count = kx2 // 2
-    groups = waves // GROUP
     span = rank * PACK
     wide = GROUP * rank
 
@@ -265,15 +265,15 @@
         return pl.BlockSpec(a.shape, lambda g: (0,) * a.ndim)
 
     return pl.pallas_call(
-        mix_kernel,
+        functools.partial(mix_kernel, base),
         grid=(groups,),
         in_specs=[
             whole(arrived), whole(height), whole(lift), whole(row_sum), whole(bias_row),
-            pl.BlockSpec((rank, channels, wide), lambda g: (0, 0, g)),
+            pl.BlockSpec((rank, channels, wide), lambda g: (0, 0, base + g)),
             whole(first), whole(back), whole(spread),
         ],
         out_specs=pl.BlockSpec((kx2, GROUP * channels), lambda g: (0, g)),
-        out_shape=jax.ShapeDtypeStruct((kx2, waves * channels), jnp.bfloat16),
+        out_shape=jax.ShapeDtypeStruct((kx2, groups * GROUP * channels), jnp.bfloat16),
         scratch_shapes=[
             pltpu.VMEM((variables * waves, height.shape[1]), jnp.bfloat16),
             pltpu.VMEM((groups, kx2, GROUP * channels), jnp.bfloat16),
@@ -284,11 +284,15 @@
             pltpu.VMEM((kx2, rank * wide), jnp.bfloat16),
         ],
         compiler_params=pltpu.CompilerParams(vmem_limit_bytes=48 * 2**20),
+        cost_estimate=pl.CostEstimate(
+            flops=groups * 7 * 10**9, bytes_accessed=8 * 2**20, transcendentals=0
+        ),
         name="mix",
     )(arrived, height, lift, row_sum, bias_row, joined, first, back, spread)
 
 
-def rows_kernel(table, gathered, cols, turned):
+def rows_kernel(table, gathered, *rest):
+    cols, turned = rest[-2:]
     row_count, waves, channels = turned.shape
     for p in range(2):
         got = dense(table[p * row_count:(p + 1) * row_count, :], gathered[0])
@@ -297,50 +301,61 @@
         cols[:, p] = turned[...].astype(jnp.bfloat16)
 
 
-def rows_back(table, gathered, waves):
+def rows_back(table, gathered, channels, half, halves, earlier):
     holders, kx2, flat = gathered.shape
     row_count = table.shape[0] // 2
-    channels = flat // waves
+    waves = flat // channels
+    shape = (row_count, 2, holders * halves * waves, channels)
+    extra = [] if earlier is None else [earlier]
     return pl.pallas_call(
         rows_kernel,
         grid=(holders,),
         in_specs=[
             pl.BlockSpec(table.shape, lambda d: (0, 0)),
             pl.BlockSpec((1, kx2, flat), lambda d: (d, 0, 0)),
-        ],
-        out_specs=pl.BlockSpec((row_count, 2, waves, channels), lambda d: (0, 0, d, 0)),
-        out_shape=jax.ShapeDtypeStruct((row_count, 2, holders * waves, channels), jnp.bfloat16),
+        ] + [pl.BlockSpec(memory_space=pl.ANY) for _ in extra],
+        input_output_aliases={2: 0} if extra else {},
+        cost_estimate=pl.CostEstimate(
+            flops=2 * holders * kx2 * kx2 * flat, bytes_accessed=16 * 2**20, transcendentals=0
+        ),
+        out_specs=pl.BlockSpec((row_count, 2, waves, channels), lambda d: (0, 0, d * halves + half, 0)),
+        out_shape=jax.ShapeDtypeStruct(shape, jnp.bfloat16),
         scratch_shapes=[pltpu.VMEM((row_count, waves, channels), jnp.float32)],
         compiler_params=pltpu.CompilerParams(vmem_limit_bytes=48 * 2**20),
         name="rows_back",
-    )(table, gathered)
-
-
-LANES = 256
+    )(table, gathered, *extra)
+
+
+LANES = 512
+HALF = PACK // 2
 
 
 def gelu(h):
     return h * (0.5 + 0.5 * lax.erf(h * (1.0 / math.sqrt(2.0))))
 
 
-def finish_kernel(fields, cols, width, skip, bias, closing, out_bias, result, turned, active):
+def finish_kernel(fields, cols, width, skip, bias, closing, out_bias, result, turned, source, active):
     variables, rows, points = fields.shape
     channels = cols.shape[2]
     for x in range(rows):
         turned[x * channels:(x + 1) * channels, :] = cols[x].T
+    for h in range(2):
+        source[h] = fields[:, h * HALF:(h + 1) * HALF, :].reshape(variables * HALF, points)
 
     def step(i, carry):
         start = pl.multiple_of(i * LANES, LANES)
         lanes = pl.ds(start, LANES)
-        source = fields[:, :, lanes].reshape(variables * rows, LANES)
         table = width[:, lanes]
         depth = 2 * channels
-        for x in range(rows // 2):
-            here = slice(x * depth, (x + 1) * depth)
-            total = dense(turned[here, :], table) + dense(skip[here, :], source) + bias[here, :]
-            active[here, :] = gelu(total).astype(jnp.bfloat16)
-        got = dense(closing[...], active[...]) + out_bias[...]
-        result[:, :, lanes] = got.astype(jnp.bfloat16).reshape(variables, rows, LANES)
+        for h in range(2):
+            near = source[h, :, lanes]
+            for x in range(HALF // 2):
+                here = slice(x * depth, (x + 1) * depth)
+                top = h * HALF * channels + x * depth
+                total = dense(turned[top:top + depth, :], table) + dense(skip[here, :], near) + bias[here, :]
+                active[here, :] = gelu(total).astype(jnp.bfloat16)
+            got = dense(closing[...], active[...]) + out_bias[...]
+            result[:, h * HALF:(h + 1) * HALF, lanes] = got.reshape(variables, HALF, LANES).astype(jnp.bfloat16)
         return carry
 
     lax.fori_loop(0, points // LANES, step, 0)
@@ -365,7 +380,8 @@
         out_shape=jax.ShapeDtypeStruct(fields.shape, jnp.bfloat16),
         scratch_shapes=[
             pltpu.VMEM((PACK * channels, depth), jnp.bfloat16),
-            pltpu.VMEM((PACK * channels, LANES), jnp.bfloat16),
+            pltpu.VMEM((2, variables * HALF, points), jnp.bfloat16),
+            pltpu.VMEM((HALF * channels, LANES), jnp.bfloat16),
         ],
         compiler_params=pltpu.CompilerParams(vmem_limit_bytes=48 * 2**20),
         name="finish",
@@ -374,6 +390,7 @@
 
 def gather_factors(first_core, input_core, output_core):
     count, rank, _ = first_core.shape
+    first_core = first_core.reshape(count // PACK, PACK, rank, rank).transpose(0, 2, 1, 3)
     flat = jnp.concatenate(
         [first_core.reshape(-1), input_core.reshape(-1), output_core.reshape(-1)]
     ).reshape(-1, 128)
@@ -381,7 +398,7 @@
     parts = whole.shape[0]
     size = first_core.size
     whole = whole.reshape(parts, -1)
-    first = whole[:, :size].reshape(parts * count, rank, rank)
+    first = whole[:, :size].reshape(-1, rank)
     inner = whole[:, size:2 * size].reshape(parts * count, rank, rank)
     outer = whole[:, 2 * size:].reshape(parts * count, 2, rank, rank)
     return first, inner, outer
@@ -437,25 +454,32 @@
     joined = jnp.einsum(
         "mbd,cde->bcme", second_core, inner, preferred_element_type=jnp.float32
     ).astype(jnp.bfloat16).reshape(rank, channels, waves * rank)
-    packed = first.reshape(MX // PACK, PACK, rank, rank).transpose(0, 2, 1, 3).reshape(-1, rank)
     back = outer.transpose(3, 2, 1, 0).reshape(rank * rank, -1)
     spread = jnp.asarray(np.repeat(np.eye(rank), PACK, axis=1).astype(ml_dtypes.bfloat16))
-    mixed = mix(
-        arrived, jnp.asarray(height), lift, jnp.asarray(row_sum), bias_row, joined, packed, back, spread
-    )
-    gathered = lax.all_gather(mixed, ("mode", "cores"), axis=0, tiled=False)
-    cols = rows_back(back_rows, gathered, waves).reshape(row_count, 2 * MY, channels)
+    halves = 2
+    groups = waves // GROUP // halves
+    row_sum = jnp.asarray(row_sum)
+    height = jnp.asarray(height)
+    mixed = [
+        mix(h * groups, groups, arrived, height, lift, row_sum, bias_row, joined, first, back, spread)
+        for h in range(halves)
+    ]
+    gathered = [lax.all_gather(m, ("mode", "cores"), axis=0, tiled=False) for m in mixed]
+    cols = None
+    for h in range(halves):
+        cols = rows_back(back_rows, gathered[h], channels, h, halves, cols)
+    cols = cols.reshape(row_count, 2 * MY, channels)
 
     skip_wide = skip_weight.astype(jnp.float32)
     direct = jnp.dot(lift_weight.astype(jnp.float32), skip_wide, precision="highest")
     total_bias = jnp.dot(lift_bias, skip_wide, precision="highest") + skip_bias
-    rows_eye = jnp.eye(PACK, dtype=jnp.float32)
+    rows_eye = jnp.eye(HALF, dtype=jnp.float32)
     skip = (rows_eye[:, None, None, :] * direct.T[None, :, :, None]).astype(jnp.bfloat16)
-    skip = skip.reshape(PACK * channels, variables * PACK)
+    skip = skip.reshape(HALF * channels, variables * HALF)
     closing = out_weight.T[:, None, None, :] * rows_eye.astype(jnp.bfloat16)[None, :, :, None]
-    closing = closing.reshape(variables * PACK, PACK * channels)
-    bias = jnp.tile(total_bias, PACK)[:, None]
-    last_bias = jnp.repeat(out_bias, PACK)[:, None]
+    closing = closing.reshape(variables * HALF, HALF * channels)
+    bias = jnp.tile(total_bias, HALF)[:, None]
+    last_bias = jnp.repeat(out_bias, HALF)[:, None]
     return finish(fields, cols, width, skip, bias, closing, last_bias)[None]
 
 
@@ -474,7 +498,7 @@
         P(),
     )
     holders = mesh.shape["mode"] * mesh.shape["cores"]
-    fits = MY // holders % PACK == 0 and NX // holders % 128 == 0
+    fits = MX // mesh.shape["batch"] % PACK == 0 and MY // holders % PACK == 0 and NX // holders % 128 == 0
     return jax.shard_map(
         fast_shards if fits else shards,
         mesh=mesh,

time: 222 us -> 219 us (0.986)
  Pallas kernels: 88.9 us -> 80 us
  local copies, waits for them, and re-layouts: 40.9 us -> 48.7 us
  waiting for transfers between devices: 65.5 us -> 63.2 us
    pallas_call x1, Pallas kernels: 47.7 us -> 34.3 us  [finish(): pl.pallas_call(finish_kernel, grid=(row_count // PACK,), in_specs=[pl.Blo...]
    unnamed x37 -> x36, local copies, waits for them, and re-layouts: 6.83 us -> 12.9 us
    pallas_call x1 -> x2, Pallas kernels: 26.1 us -> 30.2 us  [mix(): pl.pallas_call(functools.partial(mix_kernel, base), grid=(groups,), in_sp...]
    reshape x2, local copies, waits for them, and re-layouts: 1.89 us -> 5.85 us  [gather_factors(): inner = whole[:, size:2 * size].reshape(parts * count, rank, rank)]
    reshape x0 -> x2, local copies, waits for them, and re-layouts: none -> 3.74 us  [the longest x1 2.68 us: gather_factors(): first = whole[:, :size].reshape(-1, rank)]
    all_gather x1 -> x2, waiting for transfers between devices: 48.5 us -> 45.1 us  [fast_shards(): lax.all_gather(m, ('mode', 'cores'), axis=0, tiled=False)]
    pallas_call x1 -> x2, Pallas kernels: 15.1 us -> 15.6 us  [rows_back(): pl.pallas_call(rows_kernel, grid=(holders,), in_specs=[pl.BlockSpec(table...]
  transfers between devices with their start and end apart: 3 -> 4, of which waited for: 2 -> 3; matrix products, arithmetic and copies ran while one was open for 19% -> 20% of each run, Pallas kernels for 0% -> 11%
where the time goes in v2:
time: 219 us; the launch traced here: 218 us
  Pallas kernels  80 us (37%)
  waiting for transfers between devices  63.2 us (29%)
  local copies, waits for them, and re-layouts  48.7 us (22%)
  between operations  13.4 us (6%)
  matrix products  6.67 us (3%)
  starting transfers between devices  5.25 us (2%)
    all_gather x2, waiting for transfers between devices, fast_shards(): lax.all_gather(m, ('mode', 'cores'), axis=0, tiled=False)  45.1 us
    pallas_call x1, Pallas kernels, finish(): pl.pallas_call(finish_kernel, grid=(row_count // PACK,), in_specs=[pl.Blo...  34.3 us
    pallas_call x2, Pallas kernels, mix(): pl.pallas_call(functools.partial(mix_kernel, base), grid=(groups,), in_sp...  30.2 us
    all_gather x1, waiting for transfers between devices, gather_factors(): whole = lax.all_gather(flat, 'batch', axis=0, tiled=False)  18.1 us
    pallas_call x2, Pallas kernels, rows_back(): pl.pallas_call(rows_kernel, grid=(holders,), in_specs=[pl.BlockSpec(table...  15.6 us
    unnamed x36, local copies, waits for them, and re-layouts  12.9 us
    reshape x1, local copies, waits for them, and re-layouts, fast_shards(): joined = jnp.einsum('mbd,cde->bcme', second_core, inner, preferred_elemen...  6.46 us
    reshape x2, local copies, waits for them, and re-layouts, gather_factors(): inner = whole[:, size:2 * size].reshape(parts * count, rank, rank)  5.85 us
  transfers between devices with their start and end apart: 4, of which 3 were waited for; matrix products, arithmetic and copies ran while one was open for 20% of the time, Pallas kernels for 11%

profile of v2, /device:TPU:0, one launch (start us, length us, event | category | flops | bytes accessed | tf_op | source)
XLA Modules:
  0.0 218.5 jit_solution(5945405289241396066)
XLA Ops:
  6.5 1.4 reshape.112
  8.0 1.2 reshape.111
  9.1 1.1 copy.59
  11.1 4.2 %convolution_convert_fusion = bf16[256,20,128]{2,0,1:T(8,128)(2,1)S(1)} fusion(bf16[256,1024,1]{1,0,2:T(8,128)(2,1)} %constant.42, bf16[1,20,128,1024]{3,2,1,0:T(8,128)(2,1)} %param.17), kind=kOutput, calls=%fused_computation.1 | convolution fusion | flops 1342832640 | bytes 7077888 | tf_op jit(solution)/shard_map/ry,vxy->rvx/dot_general | solution.py:441
  16.3 1.7 reshape.108
  17.9 5.2 %all-to-all-start = ((bf16[8,32,2560]{2,1,0:T(8,128)(2,1)}), bf16[8,32,2560]{2,1,0:T(8,128)(2,1)S(1)}, u32[]{:S(2)}, u32[]{:S(2)}) async-start(bf16[8,32,2560]{2,1,0:T(8,128)(2,1)} %reshape.108), calls=%async_computation | async-start | bytes 2621440 | tf_op jit(solution)/shard_map/all_to_all | solution.py:445
  23.8 18.1 %all-gather.6.cloned.1.call-done = bf16[4,1024,128]{2,1,0:T(8,128)(2,1)} async-done(((bf16[1,1024,128]{2,1,0:T(8,128)(2,1)}), bf16[4,1024,128]{2,1,0:T(8,128)(2,1)}) %all-gather.6.cloned.1.call-update) | async-done | bytes 1048592 | tf_op jit(solution)/shard_map/all_gather | solution.py:397
  41.9 2.0 copy.56
  43.9 1.0 fusion.8
  45.1 2.6 %reshape.114 = bf16[128,32,32]{2,1,0:T(8,128)(2,1)} reshape(bf16[4,32768]{1,0:T(4,128)(2,1)} %get-tuple-element.6) | data formatting | bytes 524288 | tf_op jit(solution)/shard_map/reshape | solution.py:402
  47.7 3.3 %copy.43 = bf16[128,32,32,1]{0,1,3,2:T(8,128)(2,1)} copy(bf16[128,32,32,1]{2,1,0,3:T(8,128)(2,1)} %bitcast.80) | data formatting | bytes 524288 | tf_op jit(solution)/shard_map/reshape | solution.py:402
  51.0 2.2 convert_bitcast_fusion
  53.2 4.7 %copy.36 = bf16[32,128,16,32]{1,3,2,0:T(8,128)(2,1)} copy(bf16[32,128,16,32]{1,0,2,3:T(8,128)(2,1)S(1)} %convert_bitcast_fusion) | data formatting | bytes 8388608 | tf_op jit(solution)/shard_map/convert_element_type | solution.py:456
  57.9 6.5 %copy.38.joined = bf16[32,128,512]{2,1,0:T(8,128)(2,1)} copy(bf16[32,128,512]{1,2,0:T(8,128)(2,1)} %bitcast.76) | data formatting | bytes 8388608 | tf_op jit(solution)/shard_map/reshape | solution.py:456
  64.3 2.7 %reshape.116.first = bf16[4096,32]{1,0:T(8,128)(2,1)} reshape(bf16[4,32768]{1,0:T(4,128)(2,1)} %get-tuple-element.5) | data formatting | bytes 524288 | tf_op jit(solution)/shard_map/reshape | solution.py:401
  67.0 2.6 %reshape.117 = bf16[128,2,32,32]{3,2,1,0:T(8,128)(2,1)} reshape(bf16[4,65536]{1,0:T(4,128)(2,1)S(1)} %slice.14) | data formatting | bytes 1048576 | tf_op jit(solution)/shard_map/reshape | solution.py:403
  69.6 4.5 %copy.37 = bf16[32,32,2,128]{3,2,1,0:T(2,128)(2,1)} copy(bf16[32,32,2,128]{0,1,2,3:T(8,128)(2,1)} %bitcast.77) | data formatting | bytes 1048576 | tf_op jit(solution)/shard_map/transpose | solution.py:457
  74.1 1.1 copy.57
  75.3 1.2 copy-done.3
  76.5 1.2 copy-done.6
  77.7 15.0 %mix.3 = bf16[256,1024]{1,0:T(8,128)(2,1)} custom-call(bf16[8,32,2560]{2,1,0:T(8,128)(2,1)S(1)} %all-to-all-done.arrived, bf16[256,2048]{1,0:T(8,128)(2,1)S(1)} %copy-done.6, bf16[320,2048]{1,0:T(8,128)(2,1)S(1)} %bitcast.69, f32[256,1]{1,0:T(8,128)S(1)} %copy-done.8, f32[1,2048]{1,0:T(1,128)S(1)} %bitcast.73, bf16[32,128,512]{2,1,0:T(8,128)(2,1)} %copy.38.joined, ...), custom_call_target="tpu_custom_call" | custom-call | flops 14000000000 | bytes 8388608 | tf_op jit(solution)/shard_map/mix/pallas_call | solution.py:267
  92.8 1.2 copy-done.4
  94.0 1.2 copy-done.7
  95.2 15.2 %mix.2 = bf16[256,1024]{1,0:T(8,128)(2,1)} custom-call(bf16[8,32,2560]{2,1,0:T(8,128)(2,1)S(1)} %all-to-all-done.arrived, bf16[256,2048]{1,0:T(8,128)(2,1)S(1)} %copy-done.7, bf16[320,2048]{1,0:T(8,128)(2,1)S(1)} %bitcast.70, f32[256,1]{1,0:T(8,128)S(1)} %copy-done.8, f32[1,2048]{1,0:T(1,128)S(1)} %bitcast.74, bf16[32,128,512]{2,1,0:T(8,128)(2,1)} %copy.38.joined, ...), custom_call_target="tpu_custom_call" | custom-call | flops 14000000000 | bytes 8388608 | tf_op jit(solution)/shard_map/mix/pallas_call | solution.py:267
  111.6 0.9 dynamic-slice_bitcast_fusion.table
  112.7 16.4 %all-gather.10.cloned.1.call-done = bf16[2048,1024]{1,0:T(8,128)(2,1)} async-done(((bf16[256,1024]{1,0:T(8,128)(2,1)}), bf16[2048,1024]{1,0:T(8,128)(2,1)}) %all-gather.10.cloned.1.call-update) | async-done | bytes 4194320 | tf_op jit(solution)/shard_map/all_gather | solution.py:467
  129.1 2.2 %copy-done.1 = bf16[2048,1024]{1,0:T(8,128)(2,1)S(1)} copy-done((bf16[2048,1024]{1,0:T(8,128)(2,1)S(1)}, bf16[2048,1024]{1,0:T(8,128)(2,1)}, u32[]{:S(2)}) %copy-start.1) | copy-done | bytes 4194328
  131.3 7.8 %rows_back.2.rest_0_ = bf16[128,2,128,128]{3,2,1,0:T(8,128)(2,1)} custom-call(bf16[256,256]{1,0:T(8,128)(2,1)S(1)} %dynamic-slice_bitcast_fusion.table, bf16[8,256,1024]{2,1,0:T(8,128)(2,1)S(1)} %bitcast.67), custom_call_target="tpu_custom_call" | custom-call | flops 1073741824 | bytes 16777216 | tf_op jit(solution)/shard_map/rows_back/pallas_call | solution.py:310
  139.1 28.7 %all-gather.8.cloned.1.call-done = bf16[2048,1024]{1,0:T(8,128)(2,1)} async-done(((bf16[256,1024]{1,0:T(8,128)(2,1)}), bf16[2048,1024]{1,0:T(8,128)(2,1)}) %all-gather.8.cloned.1.call-update) | async-done | bytes 4194320 | tf_op jit(solution)/shard_map/all_gather | solution.py:467
  167.7 2.2 %copy-done.2 = bf16[2048,1024]{1,0:T(8,128)(2,1)S(1)} copy-done((bf16[2048,1024]{1,0:T(8,128)(2,1)S(1)}, bf16[2048,1024]{1,0:T(8,128)(2,1)}, u32[]{:S(2)}) %copy-start.2) | copy-done | bytes 4194328
  169.9 7.8 %rows_back.3 = bf16[128,2,128,128]{3,2,1,0:T(8,128)(2,1)} custom-call(bf16[256,256]{1,0:T(8,128)(2,1)S(1)} %dynamic-slice_bitcast_fusion.table, bf16[8,256,1024]{2,1,0:T(8,128)(2,1)S(1)} %bitcast.68, bf16[128,2,128,128]{3,2,1,0:T(8,128)(2,1)} %rows_back.2.rest_0_), custom_call_target="tpu_custom_call", output_to_operand_aliasing={{}: (2, {})} | custom-call | flops 1073741824 | bytes 16777216 | tf_op jit(solution)/shard_map/rows_back/pallas_call | solution.py:310
  177.7 34.3 %finish.1 = bf16[20,128,1024]{2,1,0:T(8,128)(2,1)} custom-call(bf16[20,128,1024]{2,1,0:T(8,128)(2,1)} %bitcast.79, bf16[128,256,128]{2,1,0:T(8,128)(2,1)} %bitcast.75, bf16[256,1024]{1,0:T(8,128)(2,1)S(1)} %copy-done.5, bf16[1024,160]{1,0:T(8,128)(2,1)S(1)} %copy.40.skip, f32[1024,1]{1,0:T(8,128)S(1)} %copy.41.bias, ...), custom_call_target="tpu_custom_call" | custom-call | tf_op jit(solution)/shard_map/finish/pallas_call | solution.py:371
  (55 shorter events, 3.9 us)
Async XLA Ops:
  6.5 44.4 %copy-start = (bf16[16,32,32]{2,1,0:T(8,128)(2,1)S(1)}, bf16[16,32,32]{2,1,0:T(8,128)(2,1)}, u32[]{:S(2)}) copy-start(bf16[16,32,32]{2,1,0:T(8,128)(2,1)} %param.21) | copy-start | bytes 98308
  6.5 35.4 %all-gather.6.cloned.1.call-start = ((), (), s32[]{:S(2)}) async-start(), calls=%async_computation.1 | async-start | bytes 1310720 | tf_op jit(solution)/shard_map/all_gather | solution.py:397
  15.3 7.8 %copy-start.11 = (bf16[20,128]{1,0:T(8,128)(2,1)S(1)}, bf16[20,128]{1,0:T(8,128)(2,1)}, u32[]{:S(2)}) copy-start(bf16[20,128]{1,0:T(8,128)(2,1)} %param.18) | copy-start | bytes 15364
  16.2 7.5 %copy-start.14 = (f32[128]{0:T(128)S(1)}, f32[128]{0:T(128)}, u32[]{:S(2)}) copy-start(f32[128]{0:T(128)} %param.19) | copy-start | bytes 1540
  17.9 57.3 %all-to-all-start = ((bf16[8,32,2560]{2,1,0:T(8,128)(2,1)}), bf16[8,32,2560]{2,1,0:T(8,128)(2,1)S(1)}, u32[]{:S(2)}, u32[]{:S(2)}) async-start(bf16[8,32,2560]{2,1,0:T(8,128)(2,1)} %reshape.108), calls=%async_computation | async-start | bytes 2621440 | tf_op jit(solution)/shard_map/all_to_all | solution.py:445
  23.1 106.0 %all-gather.10.cloned.1.call-start = ((), (), s32[]{:S(2)}) async-start(), calls=%async_computation.3 | async-start | bytes 4718592 | tf_op jit(solution)/shard_map/all_gather | solution.py:467
  64.3 10.9 %copy-start.8 = (f32[256,1]{1,0:T(8,128)S(1)}, f32[256,1]{1,0:T(8,128)}, u32[]{:S(2)}) copy-start(f32[256,1]{1,0:T(8,128)} %constant.38.clone.row_sum) | copy-start | bytes 3076
  64.3 10.9 %copy-start.9 = (bf16[32,512]{1,0:T(8,128)(2,1)S(1)}, bf16[32,512]{1,0:T(8,128)(2,1)}, u32[]{:S(2)}) copy-start(bf16[32,512]{1,0:T(8,128)(2,1)} %constant.37.clone.spread) | copy-start | bytes 98308
  75.3 1.2 copy-start.3
  76.5 1.2 copy-start.6
  92.7 75.0 %all-gather.8.cloned.1.call-start = ((), (), s32[]{:S(2)}) async-start(), calls=%async_computation.2 | async-start | bytes 4718592 | tf_op jit(solution)/shard_map/all_gather | solution.py:467
  92.8 1.2 copy-start.4
  94.0 1.2 copy-start.7
  95.2 15.3 %copy-start.10 = (bf16[128,128]{1,0:T(8,128)(2,1)S(1)}, bf16[128,128]{1,0:T(8,128)(2,1)}, u32[]{:S(2)}) copy-start(bf16[128,128]{1,0:T(8,128)(2,1)} %param.24) | copy-start | bytes 98308
  95.2 15.8 %copy-start.15 = (f32[128]{0:T(128)S(1)}, f32[128]{0:T(128)}, u32[]{:S(2)}) copy-start(f32[128]{0:T(128)} %param.25) | copy-start | bytes 1540
  95.2 16.2 %copy-start.13 = (f32[20]{0:T(128)S(1)}, f32[20]{0:T(128)}, u32[]{:S(2)}) copy-start(f32[20]{0:T(128)} %param.27) | copy-start | bytes 244
  95.2 17.3 %copy-start.12 = (bf16[128,20]{0,1:T(8,128)(2,1)S(1)}, bf16[128,20]{0,1:T(8,128)(2,1)}, u32[]{:S(2)}) copy-start(bf16[128,20]{0,1:T(8,128)(2,1)} %param.26) | copy-start | bytes 15364
  129.1 2.2 %copy-start.1 = (bf16[2048,1024]{1,0:T(8,128)(2,1)S(1)}, bf16[2048,1024]{1,0:T(8,128)(2,1)}, u32[]{:S(2)}) copy-start(bf16[2048,1024]{1,0:T(8,128)(2,1)} %all-gather.10.cloned.1.call-done) | copy-start | bytes 12582916
  167.7 2.2 %copy-start.2 = (bf16[2048,1024]{1,0:T(8,128)(2,1)S(1)}, bf16[2048,1024]{1,0:T(8,128)(2,1)}, u32[]{:S(2)}) copy-start(bf16[2048,1024]{1,0:T(8,128)(2,1)} %all-gather.8.cloned.1.call-done) | copy-start | bytes 12582916
  169.9 7.8 %copy-start.5 = (bf16[256,1024]{1,0:T(8,128)(2,1)S(1)}, bf16[256,1024]{1,0:T(8,128)(2,1)}, u32[]{:S(2)}) copy-start(bf16[256,1024]{1,0:T(8,128)(2,1)} %constant.35.clone.width) | copy-start | bytes 1572868
Sparse Core Ops, SparseCore 0:
  11.2 30.6 all-gather.5
  92.8 36.1 all-gather.9
  131.0 36.7 all-gather.7
